TPU v7x, 256 devices: a whole 4x4x8 slice. The times are simulated.
256 devices in a mesh: sample: 2 (over z_hi), space: 8 (over y, core), filt: 16 (over z_lo, x).
Axes of the slice: x: 4, y: 4, z: 8 (z_hi: 2, z_lo: 4; z = z_hi * 4 + z_lo), core: 2. Of those that a mesh axis runs over, the one named last changes fastest.
Arguments:
- act_in: bfloat16 [2, 64, 16, 16, 128], P('sample', None, 'space'), may hold values from -6 to 6
- w_first: bfloat16 [27, 64, 128], P(None, None, 'filt'), may hold values from -0.15625 to 0.15625
- w_second: bfloat16 [27, 128, 128], P(None, None, 'filt'), may hold values from -0.109375 to 0.109375
- grad_out: bfloat16 [2, 128, 16, 16, 128], P('sample', 'filt', 'space'), may hold values from -6 to 6
Outputs:
- y_out: bfloat16 [2, 128, 16, 16, 128], P('sample', 'filt', 'space')
- grad_w_first: float32 [27, 64, 128], P(None, None, 'filt')
- grad_w_second: float32 [27, 128, 128], P(None, None, 'filt')
All inputs are finite; a program needn't handle non-finite values.
Results may differ from a plain program's by a relative error of at most 0.0054.
Values may be sent and summed in bfloat16 or wider, within the bound.
No kernel may reach another device: no remote copies, remote signals or barrier semaphores. Data moves between devices by JAX's collectives and lax.ppermute only.
A program may use at most 64 MiB of HBM per device.

v0:
```python
import math
import jax
import jax.numpy as jnp
from jax import lax
from jax.sharding import PartitionSpec as P


def padded(cells, sides, width):
    for axis, dim in sides:
        count = lax.axis_size(axis)
        ends = count - 1
        head = lax.slice_in_dim(cells, 0, width, axis=dim)
        tail = lax.slice_in_dim(cells, cells.shape[dim] - width, cells.shape[dim], axis=dim)
        cells = jnp.concatenate(
            [
                lax.ppermute(tail, axis, [(i, (i + 1) % count) for i in range(ends)]),
                cells,
                lax.ppermute(head, axis, [((i + 1) % count, i) for i in range(ends)]),
            ],
            axis=dim,
        )
    return cells


def correlate(source, kernel, rim_pad):
    taps = kernel.reshape(3, 3, 3, kernel.shape[1], kernel.shape[2])
    return lax.conv_general_dilated(
        source[None],
        taps,
        (1, 1, 1),
        ((0, 0), (rim_pad, rim_pad), (1, 1)),
        dimension_numbers=("NCDHW", "DHWIO", "NCDHW"),
        preferred_element_type=jnp.float32,
    )[0]


def transpose_correlate(gradient, kernel, rim_pad):
    taps = kernel.reshape(3, 3, 3, kernel.shape[1], kernel.shape[2])[::-1, ::-1, ::-1]
    return lax.conv_general_dilated(
        gradient[None],
        taps,
        (1, 1, 1),
        ((0, 0), (rim_pad, rim_pad), (1, 1)),
        dimension_numbers=("NCDHW", "DHWOI", "NCDHW"),
        preferred_element_type=jnp.float32,
    )[0]


def kernel_gradient(source, gradient, rim_pad):
    result = lax.conv_general_dilated(
        source[None],
        gradient[None],
        (1, 1, 1),
        ((0, 0), (rim_pad, rim_pad), (1, 1)),
        dimension_numbers=("CNDHW", "IODHW", "NCDHW"),
        preferred_element_type=jnp.float32,
    )
    return jnp.transpose(result, (2, 3, 4, 0, 1)).reshape(27, source.shape[0], gradient.shape[0])


def silu_slope(value):
    logistic = jax.nn.sigmoid(value)
    return logistic * (1.0 + value * (1.0 - logistic))


def local(act_in, w_first, w_second, grad_out):
    depth_rows = act_in.shape[2]
    height = act_in.shape[3]
    width = act_in.shape[4]
    n_space = lax.axis_size("space")
    n_sample = lax.axis_size("sample")
    slab = act_in[0]
    padded_in = padded(slab, (("space", 1),), 2)
    row_ids = lax.axis_index("space") * depth_rows - 1 + jnp.arange(depth_rows + 2, dtype=jnp.int32)
    inside = (row_ids >= 0) & (row_ids < depth_rows * n_space)
    z_first = correlate(padded_in, w_first, 1)
    act_ext = jnp.where(inside[None, :, None, None], jax.nn.silu(z_first), 0.0).astype(jnp.bfloat16)
    gathered = lax.all_gather(act_ext, "filt", axis=0, tiled=True)
    z_second = correlate(gathered, w_second, 1)
    y_local = jax.nn.silu(z_second).astype(jnp.bfloat16)
    grad_second = (grad_out[0].astype(jnp.float32) * silu_slope(z_second)).astype(jnp.bfloat16)
    grad_rim = padded(grad_second, (("space", 1),), 1)
    back_own = lax.psum_scatter(
        transpose_correlate(grad_rim, w_second, 1), "filt", scatter_dimension=0, tiled=True
    )
    dw_second = kernel_gradient(gathered, grad_second, 1)
    grad_first = (back_own * silu_slope(z_first[:, 1:-1])).astype(jnp.bfloat16)
    dw_first = kernel_gradient(padded_in[:, 1:-1], grad_first, 1)
    sum_first, sum_second = lax.psum((dw_first, dw_second), ("sample", "space"))
    factor = 1.0 / math.sqrt(n_sample * depth_rows * n_space * height * width)
    return (y_local[None], sum_first * factor, sum_second * factor)


def solution(mesh):
    placed = (
        P("sample", None, "space", None, None),
        P(None, None, "filt"),
        P(None, None, "filt"),
        P("sample", "filt", "space", None, None),
    )
    return jax.shard_map(
        local,
        mesh=mesh,
        in_specs=placed,
        out_specs=(
            P("sample", "filt", "space", None, None),
            P(None, None, "filt"),
            P(None, None, "filt"),
        ),
        check_vma=False,
    )
```

profile of v0, /device:TPU:0, one launch (start us, length us, event | category | flops | bytes accessed | tf_op | source)
XLA Modules:
  0.0 608.5 jit_solution(2420930683141478989)
XLA Ops:
  9.9 3.3 copy.90
  13.2 2.1 copy.93
  15.3 2.1 copy.94
  17.5 2.4 pad_maximum_fusion
  21.5 18.2 %broadcast_select_fusion = f32[4,16,8,17,8]{4,2,3,1,0:T(8,128)} fusion(pred[8,17]{0,1:T(8,128)(4,1)S(1)} %copy-done.5, bf16[3,3,3,64,8]{3,4,2,1,0:T(8,128)(2,1)S(1)} %bitcast.98, bf16[64,6,16,1,7,2]{0,4,5,2,1,3:T(8,128)(2,1)S(1)} %slice.24, bf16[64,6,16,1,8,17]{0,4,5,2,1,3:T(8,128)(2,1)S(1)} %copy.96), kind=kOutput, calls=%fused_computation.27 | convolution fusion | flops 236294144 | bytes 2149512 | tf_op jit(solution)/shard_map/conv_general_dilated | solution.py:27
  39.6 6.1 %copy.97 = f32[4,16,8,17,8]{3,2,4,1,0:T(8,128)} copy(f32[4,16,8,17,8]{4,2,3,1,0:T(8,128)} %broadcast_select_fusion) | data formatting | bytes 557056 | tf_op jit(solution)/shard_map/conv_general_dilated | solution.py:27
  45.8 2.8 reshape.38
  48.5 1.7 select_convert_fusion
  50.3 80.8 %all-gather.2.cloned.1.call-done = bf16[128,4,16,128]{3,0,2,1:T(8,128)(2,1)} async-done(((bf16[8,4,16,128]{3,0,2,1:T(8,128)(2,1)}), bf16[128,4,16,128]{3,0,2,1:T(8,128)(2,1)}) %all-gather.2.cloned.1.call-update) | async-done | bytes 2097168 | tf_op jit(solution)/shard_map/all_gather | solution.py:78
  131.1 4.9 copy.127
  136.0 2.0 pad.2.clone
  138.6 9.6 %fusion.18 = f32[2,16,8,17,8]{4,2,3,1,0:T(8,128)} fusion(bf16[3,3,3,128,8]{3,4,2,1,0:T(8,128)(2,1)S(1)} %bitcast.85, bf16[128,4,16,1,7,2]{0,4,5,2,1,3:T(8,128)(2,1)S(1)} %slice.26, bf16[128,4,16,1,8,17]{0,4,5,2,1,3:T(8,128)(2,1)S(1)} %copy.100), kind=kOutput, calls=%fused_computation.20 | convolution fusion | flops 238092288 | bytes 2652160 | tf_op jit(solution)/shard_map/conv_general_dilated | solution.py:27
  148.3 3.7 copy.101
  151.9 2.9 add_multiply_fusion
  155.9 1.5 reshape.56
  157.5 2.4 copy.106
  159.9 2.2 reshape.45
  166.6 3.7 copy.117
  170.3 10.7 %copy.116 = bf16[1,128,4,16,128]{1,0,4,3,2:T(2,128)(2,1)} copy(bf16[1,128,4,16,128]{4,1,3,2,0:T(8,128)(2,1)} %bitcast.91) | data formatting | bytes 4194304 | tf_op jit(solution)/shard_map/broadcast_in_dim | solution.py:28
  181.0 31.9 %fusion.49 = f32[3,3,3,128,8]{3,4,2,1,0:T(8,128)} fusion(bf16[1,128,4,16,128]{1,0,4,3,2:T(2,128)(2,1)} %copy.116, bf16[1,8,2,16,128]{1,0,4,3,2:T(2,128)(2,1)} %copy.117), kind=kOutput, calls=%fused_computation.64 | convolution fusion | flops 215924736 | bytes 2273280 | tf_op jit(solution)/shard_map/transpose | solution.py:58
  213.2 1.7 reshape.75
  214.9 5.6 copy.109
  221.5 5.2 fusion.29
  227.2 1.4 slice.33
  228.6 3.0 copy.126
  232.7 1.7 slice_bitcast_fusion
  235.4 152.0 %all-reduce.2.cloned.1.call-done = f32[27,128,8]{1,2,0:T(8,128)} async-done(((f32[27,128,8]{1,2,0:T(8,128)}), f32[27,128,8]{1,2,0:T(8,128)}) %all-reduce.2.cloned.1.call-update) | async-done | bytes 110608 | tf_op jit(solution)/shard_map/psum | solution.py:89
  387.5 1.5 broadcast_multiply_fusion
  389.0 88.9 %reduce-scatter.2.cloned.1.call-done = f32[8,2,16,128]{3,0,2,1:T(8,128)} async-done(((f32[128,2,16,128]{3,0,2,1:T(8,128)}), f32[8,2,16,128]{3,0,2,1:T(8,128)}) %reduce-scatter.2.cloned.1.call-update) | async-done | bytes 131088 | tf_op jit(solution)/shard_map/reduce_scatter | solution.py:83
  478.8 3.7 copy.113
  482.6 33.6 %fusion.3 = f32[3,3,3,64,8]{3,4,2,1,0:T(8,128)S(1)} fusion(bf16[1,8,2,16,128]{1,0,4,3,2:T(2,128)(2,1)} %copy.113, bf16[1,64,4,16,128]{1,3,4,2,0:T(8,128)(2,1)S(1)} %copy-done.1), kind=kOutput, calls=%fused_computation.6 | convolution fusion | flops 107962368 | bytes 1169408 | tf_op jit(solution)/shard_map/transpose | solution.py:58
  516.2 85.0 %psum.14 = f32[27,64,8]{1,2,0:T(8,128)S(1)} all-reduce(f32[27,64,8]{1,2,0:T(8,128)S(1)} %bitcast.97), channel_id=1, replica_groups=mesh['sample'=2,'space'=8,'filt'=16] {'sample','space'}, use_global_device_ids=true, to_apply=%region_1.2 | all-reduce | flops 13824 | bytes 110592 | tf_op jit(solution)/shard_map/psum | solution.py:89
  (47 shorter events, 16.0 us)
Async XLA Ops:
  7.2 131.4 %copy-start = (bf16[27,128,8]{1,2,0:T(8,128)(2,1)S(1)}, bf16[27,128,8]{1,2,0:T(8,128)(2,1)}, u32[]{:S(2)}) copy-start(bf16[27,128,8]{1,2,0:T(8,128)(2,1)} %param.6) | copy-start | bytes 165892
  7.2 123.9 %all-gather.2.cloned.1.call-start = ((), (), s32[]{:S(2)}) async-start(), calls=%async_computation.1 | async-start | bytes 2228224 | tf_op jit(solution)/shard_map/all_gather | solution.py:78
  7.2 5.9 collective-permute-start
  8.6 6.8 %collective-permute-start.1 = (bf16[64,2,16,128]{3,2,1,0:T(8,128)(2,1)}, bf16[64,2,16,128]{3,2,1,0:T(8,128)(2,1)S(1)}, u32[]{:S(2)}, u32[]{:S(2)}) collective-permute-start(bf16[64,2,16,128]{3,2,1,0:T(8,128)(2,1)} %bitcast.95), channel_id=1, source_target_pairs={{16,0},{32,16},{48,32},{64,48},{80,64},{96,80},{112,96},{17,1},{33... | collective-permute-start | bytes 1572872 | tf_op jit(solution)/shard_map/ppermute | solution.py:18
  20.5 1.0 copy-start.4
  20.5 1.0 copy-start.5
  50.3 337.2 %all-reduce.2.cloned.1.call-start = ((), (), s32[]{:S(2)}) async-start(), calls=%async_computation.3 | async-start | bytes 221184 | tf_op jit(solution)/shard_map/psum | solution.py:89
  148.3 3.7 copy-start.3
  164.0 49.0 %collective-permute-start.2 = (bf16[8,1,16,128]{3,0,2,1:T(8,128)(2,1)S(1)}, bf16[8,1,16,128]{3,0,2,1:T(8,128)(2,1)S(1)}, u32[]{:S(2)}, u32[]{:S(2)}) collective-permute-start(bf16[8,1,16,128]{3,0,2,1:T(8,128)(2,1)S(1)} %get-tuple-element.20), channel_id=1, source_target_pairs={{0,16},{16,32},{32,48},{48,64},{64,80},{80,96},{96,112},{1,17},{17... | collective-permute-start | bytes 98312 | tf_op jit(solution)/shard_map/ppermute | solution.py:16
  165.3 47.7 %collective-permute-start.3 = (bf16[8,1,16,128]{3,0,2,1:T(8,128)(2,1)S(1)}, bf16[8,1,16,128]{3,0,2,1:T(8,128)(2,1)S(1)}, u32[]{:S(2)}, u32[]{:S(2)}) collective-permute-start(bf16[8,1,16,128]{3,0,2,1:T(8,128)(2,1)S(1)} %get-tuple-element.21), channel_id=1, source_target_pairs={{16,0},{32,16},{48,32},{64,48},{80,64},{96,80},{112,96},{17,1},{33... | collective-permute-start | bytes 98312 | tf_op jit(solution)/shard_map/ppermute | solution.py:18
  212.9 264.9 %reduce-scatter.2.cloned.1.call-start = ((), (), s32[]{:S(2)}) async-start(), calls=%async_computation.2 | async-start | bytes 2228224 | tf_op jit(solution)/shard_map/reduce_scatter | solution.py:83
  231.6 2.7 copy-start.2
  234.3 248.2 %copy-start.1 = (bf16[1,64,4,16,128]{1,3,4,2,0:T(8,128)(2,1)S(1)}, bf16[1,64,4,16,128]{1,3,4,2,0:T(8,128)(2,1)}, u32[]{:S(2)}) copy-start(bf16[1,64,4,16,128]{1,3,4,2,0:T(8,128)(2,1)} %slice_bitcast_fusion) | copy-start | bytes 3145732
Sparse Core Ops, SparseCore 0:
  50.4 80.6 all-gather.1
  213.1 174.3 all-reduce.1
  390.2 87.6 reduce-scatter.1
where the time goes:
time: 613 us; the launch traced here: 609 us
  waiting for transfers between devices  322 us (53%)
  matrix products  98.5 us (16%)
  blocking collectives  85 us (14%)
  local copies, waits for them, and re-layouts  71.8 us (12%)
  between operations  14.2 us (2%)
  other arithmetic  11.9 us (2%)
    psum x1, waiting for transfers between devices, local(): sum_first, sum_second = lax.psum((dw_first, dw_second), ('sample', 'space'))  152 us
    reduce_scatter x1, waiting for transfers between devices, local(): lax.psum_scatter(transpose_correlate(grad_rim, w_second, 1), 'filt', scat...  88.9 us
    psum x1, blocking collectives, local(): sum_first, sum_second = lax.psum((dw_first, dw_second), ('sample', 'space'))  85 us
    all_gather x1, waiting for transfers between devices, local(): gathered = lax.all_gather(act_ext, 'filt', axis=0, tiled=True)  80.8 us
    transpose x2, matrix products, kernel_gradient(): jnp.transpose(result, (2, 3, 4, 0, 1))  65.5 us
    conv_general_dilated x2, matrix products, correlate(): lax.conv_general_dilated(source[None], taps, (1, 1, 1), ((0, 0), (rim_pad...  27.8 us
    conv_general_dilated x9, local copies, waits for them, and re-layouts, correlate(): lax.conv_general_dilated(source[None], taps, (1, 1, 1), ((0, 0), (rim_pad...  18.8 us
    broadcast_in_dim x3, local copies, waits for them, and re-layouts, correlate(): source[None]  13.3 us
  transfers between devices with their start and end apart: 7, of which 3 were waited for; matrix products, arithmetic and copies ran while one was open for 12% of the time, Pallas kernels for 0%

commit v1 on v0

--- a/solution.py
+++ b/solution.py
@@ -86,7 +86,7 @@
     dw_second = kernel_gradient(gathered, grad_second, 1)
     grad_first = (back_own * silu_slope(z_first[:, 1:-1])).astype(jnp.bfloat16)
     dw_first = kernel_gradient(padded_in[:, 1:-1], grad_first, 1)
-    sum_first, sum_second = lax.psum((dw_first, dw_second), ("sample", "space"))
+    sum_first, sum_second = lax.psum(lax.psum((dw_first, dw_second), "sample"), "space")
     factor = 1.0 / math.sqrt(n_sample * depth_rows * n_space * height * width)
     return (y_local[None], sum_first * factor, sum_second * factor)
 

time: 613 us -> 496 us (0.81)
  waiting for transfers between devices: 322 us -> 250 us
  blocking collectives: 85 us -> 39.2 us
    psum x1 -> x2, waiting for transfers between devices: 152 us -> 79.8 us  [the longest x1 47.7 us: local(): lax.psum(lax.psum((dw_first, dw_second), 'sample'), 'space')]
    psum x1 -> x2, blocking collectives: 85 us -> 39.2 us  [the longest x1 24.8 us: local(): lax.psum(lax.psum((dw_first, dw_second), 'sample'), 'space')]
  transfers between devices with their start and end apart: 7 -> 8, of which waited for: 3 -> 4; matrix products, arithmetic and copies ran while one was open for 12% -> 15% of each run, Pallas kernels for 0% -> 0%
where the time goes in v1:
time: 496 us; the launch traced here: 491 us
  waiting for transfers between devices  250 us (50%)
  matrix products  98.5 us (20%)
  local copies, waits for them, and re-layouts  72 us (15%)
  blocking collectives  39.2 us (8%)
  between operations  14.3 us (3%)
  other arithmetic  11.9 us (2%)
  starting transfers between devices  5.36 us (1%)
    reduce_scatter x1, waiting for transfers between devices, local(): lax.psum_scatter(transpose_correlate(grad_rim, w_second, 1), 'filt', scat...  89 us
    all_gather x1, waiting for transfers between devices, local(): gathered = lax.all_gather(act_ext, 'filt', axis=0, tiled=True)  80.7 us
    transpose x2, matrix products, kernel_gradient(): jnp.transpose(result, (2, 3, 4, 0, 1))  65.5 us
    psum x1, waiting for transfers between devices, local(): lax.psum(lax.psum((dw_first, dw_second), 'sample'), 'space')  47.7 us
    psum x1, waiting for transfers between devices, local(): lax.psum((dw_first, dw_second), 'sample')  32.1 us
    conv_general_dilated x2, matrix products, correlate(): lax.conv_general_dilated(source[None], taps, (1, 1, 1), ((0, 0), (rim_pad...  27.8 us
    psum x1, blocking collectives, local(): lax.psum(lax.psum((dw_first, dw_second), 'sample'), 'space')  24.8 us
    conv_general_dilated x9, local copies, waits for them, and re-layouts, correlate(): lax.conv_general_dilated(source[None], taps, (1, 1, 1), ((0, 0), (rim_pad...  18.9 us
  transfers between devices with their start and end apart: 8, of which 4 were waited for; matrix products, arithmetic and copies ran while one was open for 15% of the time, Pallas kernels for 0%

profile of v1, /device:TPU:0, one launch (start us, length us, event | category | flops | bytes accessed | tf_op | source)
XLA Modules:
  0.0 490.9 jit_solution(11725215078133851265)
XLA Ops:
  9.9 3.3 copy.90
  13.2 2.2 copy.93
  15.3 2.1 copy.94
  17.5 2.4 pad_maximum_fusion
  21.5 18.1 %broadcast_select_fusion = f32[4,16,8,17,8]{4,2,3,1,0:T(8,128)} fusion(pred[8,17]{0,1:T(8,128)(4,1)S(1)} %copy-done.5, bf16[3,3,3,64,8]{3,4,2,1,0:T(8,128)(2,1)S(1)} %bitcast.98, bf16[64,6,16,1,7,2]{0,4,5,2,1,3:T(8,128)(2,1)S(1)} %slice.24, bf16[64,6,16,1,8,17]{0,4,5,2,1,3:T(8,128)(2,1)S(1)} %copy.96), kind=kOutput, calls=%fused_computation.27 | convolution fusion | flops 236294144 | bytes 2149512 | tf_op jit(solution)/shard_map/conv_general_dilated | solution.py:27
  39.7 6.2 %copy.97 = f32[4,16,8,17,8]{3,2,4,1,0:T(8,128)} copy(f32[4,16,8,17,8]{4,2,3,1,0:T(8,128)} %broadcast_select_fusion) | data formatting | bytes 557056 | tf_op jit(solution)/shard_map/conv_general_dilated | solution.py:27
  45.8 2.8 reshape.38
  48.6 1.7 select_convert_fusion
  50.4 80.7 %all-gather.2.cloned.1.call-done = bf16[128,4,16,128]{3,0,2,1:T(8,128)(2,1)} async-done(((bf16[8,4,16,128]{3,0,2,1:T(8,128)(2,1)}), bf16[128,4,16,128]{3,0,2,1:T(8,128)(2,1)}) %all-gather.2.cloned.1.call-update) | async-done | bytes 2097168 | tf_op jit(solution)/shard_map/all_gather | solution.py:78
  131.1 4.9 copy.127
  136.0 2.0 pad.2.clone
  138.6 9.6 %fusion.18 = f32[2,16,8,17,8]{4,2,3,1,0:T(8,128)} fusion(bf16[3,3,3,128,8]{3,4,2,1,0:T(8,128)(2,1)S(1)} %bitcast.85, bf16[128,4,16,1,7,2]{0,4,5,2,1,3:T(8,128)(2,1)S(1)} %slice.26, bf16[128,4,16,1,8,17]{0,4,5,2,1,3:T(8,128)(2,1)S(1)} %copy.100), kind=kOutput, calls=%fused_computation.20 | convolution fusion | flops 238092288 | bytes 2652160 | tf_op jit(solution)/shard_map/conv_general_dilated | solution.py:27
  148.3 3.7 copy.101
  152.0 2.8 add_multiply_fusion
  157.5 2.4 copy.106
  159.9 2.2 reshape.45
  166.6 3.7 copy.117
  170.3 10.7 %copy.116 = bf16[1,128,4,16,128]{1,0,4,3,2:T(2,128)(2,1)} copy(bf16[1,128,4,16,128]{4,1,3,2,0:T(8,128)(2,1)} %bitcast.91) | data formatting | bytes 4194304 | tf_op jit(solution)/shard_map/broadcast_in_dim | solution.py:28
  181.1 31.9 %fusion.49 = f32[3,3,3,128,8]{3,4,2,1,0:T(8,128)} fusion(bf16[1,128,4,16,128]{1,0,4,3,2:T(2,128)(2,1)} %copy.116, bf16[1,8,2,16,128]{1,0,4,3,2:T(2,128)(2,1)} %copy.117), kind=kOutput, calls=%fused_computation.64 | convolution fusion | flops 215924736 | bytes 2273280 | tf_op jit(solution)/shard_map/transpose | solution.py:58
  213.3 1.7 reshape.75
  215.0 5.6 %copy.109 = bf16[8,4,16,1,8,17]{0,4,5,2,1,3:T(8,128)(2,1)} copy(bf16[8,4,16,1,8,17]{5,4,0,2,1,3:T(8,128)(2,1)} %reshape.75) | data formatting | bytes 278528 | tf_op jit(solution)/shard_map/conv_general_dilated | solution.py:39
  221.6 32.1 %all-reduce.3.cloned.1.call-done = f32[27,128,8]{1,2,0:T(8,128)} async-done(((f32[27,128,8]{1,2,0:T(8,128)}), f32[27,128,8]{1,2,0:T(8,128)}) %all-reduce.3.cloned.1.call-update) | async-done | bytes 110608 | tf_op jit(solution)/shard_map/psum | solution.py:89
  253.8 5.2 %fusion.29 = f32[2,16,8,17,128]{4,2,3,1,0:T(8,128)S(1)} fusion(bf16[3,3,3,128,8]{3,4,2,1,0:T(8,128)(2,1)S(1)} %bitcast.86, bf16[8,4,16,1,7,2]{0,4,5,2,1,3:T(8,128)(2,1)S(1)} %slice.32, bf16[8,4,16,1,8,17]{0,4,5,2,1,3:T(8,128)(2,1)} %copy.109, pred[8,17]{0,1:T(8,128)(4,1)S(1)} %copy-done.5), kind=kOutput, calls=%fused_computation.30 | convolution fusion | flops 231645184 | bytes 2437256 | tf_op jit(solution)/shard_map/conv_general_dilated | solution.py:39
  260.9 3.0 copy.126
  265.0 1.7 slice_bitcast_fusion
  267.7 47.7 %all-reduce.5.cloned.1.call-done = f32[27,128,8]{1,2,0:T(8,128)} async-done(((f32[27,128,8]{1,2,0:T(8,128)}), f32[27,128,8]{1,2,0:T(8,128)}) %all-reduce.5.cloned.1.call-update) | async-done | bytes 110608 | tf_op jit(solution)/shard_map/psum | solution.py:89
  315.4 1.5 broadcast_multiply_fusion
  317.0 89.0 %reduce-scatter.2.cloned.1.call-done = f32[8,2,16,128]{3,0,2,1:T(8,128)} async-done(((f32[128,2,16,128]{3,0,2,1:T(8,128)}), f32[8,2,16,128]{3,0,2,1:T(8,128)}) %reduce-scatter.2.cloned.1.call-update) | async-done | bytes 131088 | tf_op jit(solution)/shard_map/reduce_scatter | solution.py:83
  407.0 3.7 copy.113
  410.7 33.6 %fusion.3 = f32[3,3,3,64,8]{3,4,2,1,0:T(8,128)S(1)} fusion(bf16[1,8,2,16,128]{1,0,4,3,2:T(2,128)(2,1)} %copy.113, bf16[1,64,4,16,128]{1,3,4,2,0:T(8,128)(2,1)S(1)} %copy-done.1), kind=kOutput, calls=%fused_computation.6 | convolution fusion | flops 107962368 | bytes 1169408 | tf_op jit(solution)/shard_map/transpose | solution.py:58
  444.3 14.4 %psum.28 = f32[27,64,8]{1,2,0:T(8,128)S(1)} all-reduce(f32[27,64,8]{1,2,0:T(8,128)S(1)} %bitcast.97), channel_id=1, replica_groups=mesh['sample'=2,'space'=8,'filt'=16] {'sample'}, use_global_device_ids=true, to_apply=%region_1.2 | all-reduce | flops 13824 | bytes 110592 | tf_op jit(solution)/shard_map/psum | solution.py:89
  458.7 24.8 %psum.29 = f32[27,64,8]{1,2,0:T(8,128)S(1)} all-reduce(f32[27,64,8]{1,2,0:T(8,128)S(1)} %psum.28), channel_id=1, replica_groups=mesh['sample'=2,'space'=8,'filt'=16] {'space'}, use_global_device_ids=true, to_apply=%region_2.3 | all-reduce | flops 13824 | bytes 110592 | tf_op jit(solution)/shard_map/psum | solution.py:89
  (51 shorter events, 19.1 us)
Async XLA Ops:
  7.2 131.5 %copy-start = (bf16[27,128,8]{1,2,0:T(8,128)(2,1)S(1)}, bf16[27,128,8]{1,2,0:T(8,128)(2,1)}, u32[]{:S(2)}) copy-start(bf16[27,128,8]{1,2,0:T(8,128)(2,1)} %param.6) | copy-start | bytes 165892
  7.2 123.9 %all-gather.2.cloned.1.call-start = ((), (), s32[]{:S(2)}) async-start(), calls=%async_computation.1 | async-start | bytes 2228224 | tf_op jit(solution)/shard_map/all_gather | solution.py:78
  7.2 6.0 %collective-permute-start = (bf16[64,2,16,128]{3,2,1,0:T(8,128)(2,1)}, bf16[64,2,16,128]{3,2,1,0:T(8,128)(2,1)S(1)}, u32[]{:S(2)}, u32[]{:S(2)}) collective-permute-start(bf16[64,2,16,128]{3,2,1,0:T(8,128)(2,1)} %bitcast.94), channel_id=1, source_target_pairs={{0,16},{16,32},{32,48},{48,64},{64,80},{80,96},{96,112},{1,17},{17... | collective-permute-start | bytes 1572872 | tf_op jit(solution)/shard_map/ppermute | solution.py:16
  8.6 6.8 %collective-permute-start.1 = (bf16[64,2,16,128]{3,2,1,0:T(8,128)(2,1)}, bf16[64,2,16,128]{3,2,1,0:T(8,128)(2,1)S(1)}, u32[]{:S(2)}, u32[]{:S(2)}) collective-permute-start(bf16[64,2,16,128]{3,2,1,0:T(8,128)(2,1)} %bitcast.95), channel_id=1, source_target_pairs={{16,0},{32,16},{48,32},{64,48},{80,64},{96,80},{112,96},{17,1},{33... | collective-permute-start | bytes 1572872 | tf_op jit(solution)/shard_map/ppermute | solution.py:18
  20.5 1.0 copy-start.4
  20.5 1.0 copy-start.5
  50.3 203.4 %all-reduce.3.cloned.1.call-start = ((), (), s32[]{:S(2)}) async-start(), calls=%async_computation.3 | async-start | bytes 221184 | tf_op jit(solution)/shard_map/psum | solution.py:89
  148.3 3.7 copy-start.3
  164.0 49.1 %collective-permute-start.2 = (bf16[8,1,16,128]{3,0,2,1:T(8,128)(2,1)S(1)}, bf16[8,1,16,128]{3,0,2,1:T(8,128)(2,1)S(1)}, u32[]{:S(2)}, u32[]{:S(2)}) collective-permute-start(bf16[8,1,16,128]{3,0,2,1:T(8,128)(2,1)S(1)} %get-tuple-element.20), channel_id=1, source_target_pairs={{0,16},{16,32},{32,48},{48,64},{64,80},{80,96},{96,112},{1,17},{17... | collective-permute-start | bytes 98312 | tf_op jit(solution)/shard_map/ppermute | solution.py:16
  165.3 47.8 %collective-permute-start.3 = (bf16[8,1,16,128]{3,0,2,1:T(8,128)(2,1)S(1)}, bf16[8,1,16,128]{3,0,2,1:T(8,128)(2,1)S(1)}, u32[]{:S(2)}, u32[]{:S(2)}) collective-permute-start(bf16[8,1,16,128]{3,0,2,1:T(8,128)(2,1)S(1)} %get-tuple-element.21), channel_id=1, source_target_pairs={{16,0},{32,16},{48,32},{64,48},{80,64},{96,80},{112,96},{17,1},{33... | collective-permute-start | bytes 98312 | tf_op jit(solution)/shard_map/ppermute | solution.py:18
  213.0 102.4 %all-reduce.5.cloned.1.call-start = ((), (), s32[]{:S(2)}) async-start(), calls=%async_computation.4 | async-start | bytes 221184 | tf_op jit(solution)/shard_map/psum | solution.py:89
  253.7 152.3 %reduce-scatter.2.cloned.1.call-start = ((), (), s32[]{:S(2)}) async-start(), calls=%async_computation.2 | async-start | bytes 2228224 | tf_op jit(solution)/shard_map/reduce_scatter | solution.py:83
  263.9 2.7 copy-start.2
  266.6 144.1 %copy-start.1 = (bf16[1,64,4,16,128]{1,3,4,2,0:T(8,128)(2,1)S(1)}, bf16[1,64,4,16,128]{1,3,4,2,0:T(8,128)(2,1)}, u32[]{:S(2)}) copy-start(bf16[1,64,4,16,128]{1,3,4,2,0:T(8,128)(2,1)} %slice_bitcast_fusion) | copy-start | bytes 3145732
Sparse Core Ops, SparseCore 0:
  50.5 80.6 all-gather.1
  213.1 40.5 all-reduce.2
  256.0 59.3 all-reduce.4
  318.0 87.9 reduce-scatter.1
